TPU v7x, 32 devices: a whole 2x2x4 slice. The times are simulated.
32 devices in a mesh: dp: 4 (over y, x), seq: 8 (over z, core).
Axes of the slice: x: 2, y: 2, z: 4, core: 2. Of those that a mesh axis runs over, the one named last changes fastest.
Arguments:
- loaded: float32 [8, 24, 1664], P('seq', 'dp'), may hold values from -24 to 24
- tile_rows: int32 [8, 24], P('seq', 'dp'), may hold values from 0 to 23, as said below
- bucket_ids: int32 [2], replicated, may hold values from 0 to 3, as said below
- in_weight: float32 [96, 81], replicated, may hold values from -0.625 to 0.625
- in_bias: float32 [96], replicated, may hold values from -3 to 3
- bucket_bias: float32 [4, 96], replicated, may hold values from -4 to 4
- norm_gain: float32 [96], replicated, may hold values from 0.5 to 1.5
- mid_weight: float32 [27, 96, 96], replicated, may hold values from -0.125 to 0.125
- mid_bias: float32 [96], replicated, may hold values from -3 to 3
- head_gain: float32 [96], replicated, may hold values from 0.5 to 1.5
- head_weight: float32 [16, 96], replicated, may hold values from -0.625 to 0.625
- head_bias: float32 [16], replicated, may hold values from -3 to 3
Outputs:
- latent_tokens: float32 [8, 8, 26624], P(None, 'dp', 'seq')
Inputs may be any that keep to these rules, and one draw needn't show every extreme that they name: For each frame, tile_rows[g] is a permutation of the 24 tiles. The 6 entries held by one index of dp name at most 2 tiles of any one row band (band o holds tiles 6 * o to 6 * o + 5), and in every frame some index of dp names exactly 2 tiles of some band. `bucket_ids`: clips whose numbers differ by less than 4 have different buckets; clips whose numbers differ by 4 have the same one.
All inputs are finite; a program needn't handle non-finite values.
Results may differ from a plain program's by a relative error of at most 0.0003.
Values sent between devices are 32-bit elements; how exact they have to be, the bound alone decides.
No kernel may reach another device: no remote copies, remote signals or barrier semaphores. Data moves between devices by JAX's collectives and lax.ppermute only.
A program may use at most 128 MiB of HBM per device.

v0:
```python
import jax
import jax.numpy as jnp
from jax import lax
from jax.sharding import PartitionSpec as P

FRAMES = 4


EPSILON = 1e-06
PRECISE = lax.Precision.HIGHEST


def extended(cells, sides, width):
    for axis, dim in sides:
        count = lax.axis_size(axis)
        ends = count - 1
        head = lax.slice_in_dim(cells, 0, width, axis=dim)
        tail = lax.slice_in_dim(cells, cells.shape[dim] - width, cells.shape[dim], axis=dim)
        cells = jnp.concatenate(
            [
                lax.ppermute(tail, axis, [(i, (i + 1) % count) for i in range(ends)]),
                cells,
                lax.ppermute(head, axis, [((i + 1) % count, i) for i in range(ends)]),
            ],
            axis=dim,
        )
    return cells


def passed_along(block, axis, distance):
    devices = range(lax.axis_size(axis))
    route = [(i - distance, i) for i in devices if i - distance in devices]
    return lax.ppermute(block, axis, route)


def scaled_norm(values, scales):
    square = jnp.mean(values * values, axis=-2, keepdims=True)
    return values * lax.rsqrt(square + EPSILON) * scales[:, None]


def context(source, rim_rows, history, row_len, frame_pos):
    padded = extended(source, (("dp", 1),), rim_rows * row_len)
    layers = [padded]
    current = padded
    for earlier in range(history):
        current = passed_along(current, "seq", 1)
        layers.append(jnp.where(frame_pos > earlier, current, 0.0))
    return jnp.stack(layers[::-1], 0)


def entry_conv(stacked, weights, row_len):
    rows_out = stacked.shape[2] // row_len - 2
    cells_out = rows_out * row_len
    padded = jnp.pad(stacked, ((0, 0), (0, 0), (1, 1)))
    column = jnp.arange(cells_out) % row_len
    pieces = []
    for step_time in range(3):
        for step_row in range(3):
            for step_col in range(3):
                offset_at = step_row * row_len + step_col
                tap_slab = lax.slice_in_dim(
                    padded[step_time], offset_at, offset_at + cells_out, axis=1
                )
                if step_col == 0:
                    tap_slab = jnp.where(column > 0, tap_slab, 0.0)
                if step_col == 2:
                    tap_slab = jnp.where(column < row_len - 1, tap_slab, 0.0)
                pieces.append(tap_slab)
    columns_all = jnp.concatenate(pieces, 0)
    results = [jnp.dot(weights, columns_all, precision=PRECISE, preferred_element_type=jnp.float32)]
    return jnp.stack(results, 0)


def middle_conv(stacked, tap_weights, row_len):
    rows_out = stacked.shape[2] // row_len - 2
    cells_out = rows_out * row_len
    padded = jnp.pad(stacked, ((0, 0), (0, 0), (1, 1)))
    column = jnp.arange(cells_out) % row_len
    groups = []
    for step_col in range(3):
        running = jnp.zeros((tap_weights.shape[1], cells_out), jnp.float32)
        for step_time in range(3):
            for step_row in range(3):
                offset_at = step_row * row_len + step_col
                tap_slab = lax.slice_in_dim(
                    padded[step_time], offset_at, offset_at + cells_out, axis=1
                )
                running = running + jnp.dot(
                    tap_weights[step_time * 9 + step_row * 3 + step_col],
                    tap_slab,
                    precision=PRECISE,
                    preferred_element_type=jnp.float32,
                )
        groups.append(running)
    return (
        groups[1]
        + jnp.where(column > 0, groups[0], 0.0)
        + jnp.where(column < row_len - 1, groups[2], 0.0)
    )


def body(
    loaded,
    tile_rows,
    bucket_ids,
    in_weight,
    in_bias,
    bucket_bias,
    norm_gain,
    mid_weight,
    mid_bias,
    head_gain,
    head_weight,
    head_bias,
):
    groups_dp = lax.axis_size("dp")
    tiles_dev = loaded.shape[1]
    tile_len = loaded.shape[2]
    row_len = tile_len // 2
    rows_dev = 2 * tiles_dev // 3
    capacity = 2 * ((tiles_dev // 2 + groups_dp - 1) // groups_dp)
    position = tile_rows[0]
    owners = position // tiles_dev
    owner_hot = (owners[:, None] == jnp.arange(groups_dp)[None, :]).astype(jnp.int32)
    before = jnp.cumsum(owner_hot, axis=0) - owner_hot
    ranks = jnp.sum(before * owner_hot, axis=1)
    target = owners * capacity + ranks
    placing = target[None, :] == jnp.arange(groups_dp * capacity)[:, None]
    outgoing = jnp.dot(
        placing.astype(jnp.float32),
        loaded[0],
        precision=PRECISE,
        preferred_element_type=jnp.float32,
    )
    labels = jnp.sum(jnp.where(placing, (position % tiles_dev + 1)[None, :], 0), axis=1).astype(
        jnp.float32
    )
    arrived, arrived_labels = (
        lax.all_to_all(
            outgoing.reshape(groups_dp, capacity, tile_len),
            "dp",
            split_axis=0,
            concat_axis=0,
            tiled=True,
        ),
        lax.all_to_all(
            labels.reshape(groups_dp, capacity), "dp", split_axis=0, concat_axis=0, tiled=True
        ),
    )
    wanted = (jnp.arange(tiles_dev) + 1).astype(jnp.float32)
    picking = (arrived_labels.reshape(1, -1) == wanted[:, None]).astype(jnp.float32)
    pixels = jnp.dot(
        picking,
        arrived.reshape(-1, tile_len),
        precision=PRECISE,
        preferred_element_type=jnp.float32,
    )
    pixels = pixels.reshape(3, rows_dev * row_len)
    seq_pos = lax.axis_index("seq")
    frame_pos = seq_pos % FRAMES
    clip_now = seq_pos // FRAMES
    bucket_now = jnp.sum(jnp.where(jnp.arange(bucket_ids.shape[0]) == clip_now, bucket_ids, 0))
    bucket_row = jnp.sum(
        jnp.where((jnp.arange(bucket_bias.shape[0]) == bucket_now)[:, None], bucket_bias, 0.0),
        axis=0,
    )
    offset = (in_bias + bucket_row)[:, None]
    pixel_stack = context(pixels, 1, 2, row_len, frame_pos)
    entry_out = entry_conv(pixel_stack, in_weight, row_len)[0] + offset
    active = jax.nn.silu(scaled_norm(entry_out, norm_gain))
    active_stack = context(active, 1, 2, row_len, frame_pos)
    branch = middle_conv(active_stack, mid_weight, row_len)
    summed = entry_out + branch + mid_bias[:, None]
    latent = jax.nn.silu(scaled_norm(summed, head_gain))
    latent = (
        jnp.dot(head_weight, latent, precision=PRECISE, preferred_element_type=jnp.float32)
        + head_bias[:, None]
    )
    latent_chans = latent.shape[0]
    patches = latent.reshape(latent_chans, rows_dev // 2, 2, row_len // 2, 2).transpose(
        1, 3, 0, 2, 4
    )
    patches = patches.reshape(1, rows_dev // 2, row_len // 2 * latent_chans * 4)
    return lax.all_to_all(patches, "seq", split_axis=2, concat_axis=0, tiled=True)


def solution(mesh):
    return jax.shard_map(
        body,
        mesh=mesh,
        in_specs=(
            P("seq", "dp", None),
            P("seq", "dp"),
            P(),
            P(),
            P(),
            P(),
            P(),
            P(),
            P(),
            P(),
            P(),
            P(),
        ),
        out_specs=P(None, "dp", "seq"),
        check_vma=False,
    )
```

profile of v0, /device:TPU:6, one launch (start us, length us, event | category | flops | bytes accessed | tf_op | source)
XLA Modules:
  0.0 357.8 jit_solution(4580433983427556147)
XLA Ops:
  2.3 4.2 %all-to-all-start = ((f32[4,1,2]{2,1,0:T(1,128)}), f32[4,1,2]{2,1,0:T(1,128)S(1)}, u32[]{:S(2)}, u32[]{:S(2)}) async-start(f32[4,1,2]{2,1,0:T(1,128)} %bitcast.5), calls=%async_computation | async-start | bytes 4096 | tf_op jit(solution)/shard_map/all_to_all | solution.py:146
  7.9 1.6 fusion.48
  9.5 4.8 %all-to-all-start.1 = ((f32[4,2,1664]{2,1,0:T(2,128)}), f32[4,2,1664]{2,1,0:T(2,128)S(1)}, u32[]{:S(2)}, u32[]{:S(2)}) async-start(f32[4,2,1664]{2,1,0:T(2,128)} %fusion.48), calls=%async_computation.1 | async-start | bytes 106496 | tf_op jit(solution)/shard_map/all_to_all | solution.py:139
  17.1 3.5 collective-permute-start.1
  23.3 2.9 collective-permute-done
  28.6 4.7 %collective-permute-start.3 = (f32[3,4992]{1,0:T(4,128)S(1)}, f32[3,4992]{1,0:T(4,128)S(1)}, u32[]{:S(2)}, u32[]{:S(2)}) collective-permute-start(f32[3,4992]{1,0:T(4,128)S(1)} %collective-permute-done.2), channel_id=1, source_target_pairs={{0,1},{1,2},{2,3},{3,4},{4,5},{5,6},{6,7},{8,9},{9,10},{10,11},{11... | collective-permute-start | bytes 179720 | tf_op jit(solution)/shard_map/ppermute | solution.py:33
  35.3 1.9 concatenate.10
  39.1 4.3 %collective-permute-start.5 = (f32[96,832]{1,0:T(8,128)S(1)}, f32[96,832]{1,0:T(8,128)S(1)}, u32[]{:S(2)}, u32[]{:S(2)}) collective-permute-start(f32[96,832]{1,0:T(8,128)S(1)} %get-tuple-element.10), channel_id=1, source_target_pairs={{8,0},{16,8},{24,16},{9,1},{17,9},{25,17},{10,2},{18,10},{26,18},{... | collective-permute-start | bytes 958472 | tf_op jit(solution)/shard_map/ppermute | solution.py:23
  44.7 5.1 %collective-permute-done.5 = f32[96,832]{1,0:T(8,128)S(1)} collective-permute-done((f32[96,832]{1,0:T(8,128)S(1)}, f32[96,832]{1,0:T(8,128)S(1)}, u32[]{:S(2)}, u32[]{:S(2)}) %collective-permute-start.5) | collective-permute-done | bytes 319520 | tf_op jit(solution)/shard_map/ppermute | solution.py:23
  49.8 8.2 %collective-permute-done.4 = f32[96,832]{1,0:T(8,128)S(1)} collective-permute-done((f32[96,832]{1,0:T(8,128)S(1)}, f32[96,832]{1,0:T(8,128)S(1)}, u32[]{:S(2)}, u32[]{:S(2)}) %collective-permute-start.4) | collective-permute-done | bytes 319520 | tf_op jit(solution)/shard_map/ppermute | solution.py:21
  58.1 1.7 concatenate.11
  59.8 3.9 %collective-permute-start.6 = (f32[96,4992]{1,0:T(8,128)}, f32[96,4992]{1,0:T(8,128)S(1)}, u32[]{:S(2)}, u32[]{:S(2)}) collective-permute-start(f32[96,4992]{1,0:T(8,128)} %concatenate.11), channel_id=1, source_target_pairs={{0,1},{1,2},{2,3},{3,4},{4,5},{5,6},{6,7},{8,9},{9,10},{10,11},{11... | collective-permute-start | bytes 5750792 | tf_op jit(solution)/shard_map/ppermute | solution.py:33
  63.6 3.6 %collective-permute-done.6 = f32[96,4992]{1,0:T(8,128)S(1)} collective-permute-done((f32[96,4992]{1,0:T(8,128)}, f32[96,4992]{1,0:T(8,128)S(1)}, u32[]{:S(2)}, u32[]{:S(2)}) %collective-permute-start.6) | collective-permute-done | bytes 1916960 | tf_op jit(solution)/shard_map/ppermute | solution.py:33
  67.2 23.5 %collective-permute-start.7 = (f32[96,4992]{1,0:T(8,128)S(1)}, f32[96,4992]{1,0:T(8,128)S(1)}, u32[]{:S(2)}, u32[]{:S(2)}) collective-permute-start(f32[96,4992]{1,0:T(8,128)S(1)} %collective-permute-done.6), channel_id=1, source_target_pairs={{0,1},{1,2},{2,3},{3,4},{4,5},{5,6},{6,7},{8,9},{9,10},{10,11},{11... | collective-permute-start | bytes 5750792 | tf_op jit(solution)/shard_map/ppermute | solution.py:33
  90.9 3.2 collective-permute-done.7
  94.2 2.9 select_maximum_fusion
  109.9 1.5 convolution_add_fusion.2
  111.4 1.7 convolution_add_fusion.1
  117.1 1.5 convolution_add_fusion.12
  122.6 1.5 convolution_add_fusion.23
  124.1 1.9 convolution_add_fusion.22
  126.0 1.5 convolution_add_fusion.21
  127.5 1.5 convolution_add_fusion.20
  129.0 1.5 convolution_add_fusion.19
  130.4 1.5 convolution_add_fusion.18
  136.3 1.8 multiply_reduce_fusion
  139.8 15.5 %copy.31 = f32[2,416,16,2,2]{0,4,3,2,1:T(2,128)} copy(f32[2,416,16,2,2]{2,4,1,3,0:T(2,128)S(1)} %bitcast.163) | data formatting | bytes 425984 | tf_op jit(solution)/shard_map/reshape | solution.py:183
  155.8 119.6 %reduce.6 = f32[26624,2]{1,0:T(8,128)} reduce(f32[26624,1,2]{2,1,0:T(1,128)} %bitcast.160, f32[]{:T(128)} %broadcast.202), dimensions={1}, to_apply=%bitcast.152.reduce_sub_computation | reduce | bytes 425988
  275.5 12.6 %reshape.123 = f32[8,1,6656]{2,1,0:T(1,128)S(1)} reshape(f32[26624,2]{1,0:T(8,128)} %reduce.6) | data formatting | bytes 425984
  288.0 33.0 %all_to_all.29 = f32[8,1,6656]{2,1,0:T(1,128)S(1)} all-to-all(f32[8,1,6656]{2,1,0:T(1,128)S(1)} %reshape.123), channel_id=1, replica_groups=mesh['dp'=4,'seq'=8] {'seq'}, dimensions={0} | all-to-all | bytes 425984 | tf_op jit(solution)/shard_map/all_to_all | solution.py:184
  322.2 26.6 %reshape.124 = f32[26624,1,2]{2,1,0:T(1,128)} reshape(f32[8,6656]{1,0:T(8,128)S(1)} %reduce.7) | data formatting | bytes 425984
  348.8 8.7 %copy.28 = f32[1,2,8,3328]{3,1,2,0:T(2,128)} copy(f32[1,2,8,3328]{1,3,2,0:T(8,128)} %bitcast.161) | data formatting | bytes 425984 | tf_op jit(solution)/shard_map/all_to_all | solution.py:184
  (86 shorter events, 45.3 us)
Async XLA Ops:
  0.0 37.2 %copy-start = (f32[96,81]{0,1:T(8,128)S(1)}, f32[96,81]{0,1:T(8,128)}, u32[]{:S(2)}) copy-start(f32[96,81]{0,1:T(8,128)} %param.15) | copy-start | bytes 93316
  2.3 7.2 %all-to-all-start = ((f32[4,1,2]{2,1,0:T(1,128)}), f32[4,1,2]{2,1,0:T(1,128)S(1)}, u32[]{:S(2)}, u32[]{:S(2)}) async-start(f32[4,1,2]{2,1,0:T(1,128)} %bitcast.5), calls=%async_computation | async-start | bytes 4096 | tf_op jit(solution)/shard_map/all_to_all | solution.py:146
  9.5 7.2 %all-to-all-start.1 = ((f32[4,2,1664]{2,1,0:T(2,128)}), f32[4,2,1664]{2,1,0:T(2,128)S(1)}, u32[]{:S(2)}, u32[]{:S(2)}) async-start(f32[4,2,1664]{2,1,0:T(2,128)} %fusion.48), calls=%async_computation.1 | async-start | bytes 106496 | tf_op jit(solution)/shard_map/all_to_all | solution.py:139
  17.1 6.2 %collective-permute-start.1 = (f32[3,832]{1,0:T(4,128)S(1)}, f32[3,832]{1,0:T(4,128)S(1)}, u32[]{:S(2)}, u32[]{:S(2)}) collective-permute-start(f32[3,832]{1,0:T(4,128)S(1)} %get-tuple-element.51), channel_id=1, source_target_pairs={{8,0},{16,8},{24,16},{9,1},{17,9},{25,17},{10,2},{18,10},{26,18},{... | collective-permute-start | bytes 29960 | tf_op jit(solution)/shard_map/ppermute | solution.py:23
  20.6 5.6 %collective-permute-start = (f32[3,832]{1,0:T(4,128)S(1)}, f32[3,832]{1,0:T(4,128)S(1)}, u32[]{:S(2)}, u32[]{:S(2)}) collective-permute-start(f32[3,832]{1,0:T(4,128)S(1)} %get-tuple-element.52), channel_id=1, source_target_pairs={{0,8},{8,16},{16,24},{1,9},{9,17},{17,25},{2,10},{10,18},{18,26},{... | collective-permute-start | bytes 29960 | tf_op jit(solution)/shard_map/ppermute | solution.py:21
  26.4 2.2 collective-permute-start.2
  28.6 5.7 %collective-permute-start.3 = (f32[3,4992]{1,0:T(4,128)S(1)}, f32[3,4992]{1,0:T(4,128)S(1)}, u32[]{:S(2)}, u32[]{:S(2)}) collective-permute-start(f32[3,4992]{1,0:T(4,128)S(1)} %collective-permute-done.2), channel_id=1, source_target_pairs={{0,1},{1,2},{2,3},{3,4},{4,5},{5,6},{6,7},{8,9},{9,10},{10,11},{11... | collective-permute-start | bytes 179720 | tf_op jit(solution)/shard_map/ppermute | solution.py:33
  37.2 1.4 copy-start.5
  39.1 10.7 %collective-permute-start.5 = (f32[96,832]{1,0:T(8,128)S(1)}, f32[96,832]{1,0:T(8,128)S(1)}, u32[]{:S(2)}, u32[]{:S(2)}) collective-permute-start(f32[96,832]{1,0:T(8,128)S(1)} %get-tuple-element.10), channel_id=1, source_target_pairs={{8,0},{16,8},{24,16},{9,1},{17,9},{25,17},{10,2},{18,10},{26,18},{... | collective-permute-start | bytes 958472 | tf_op jit(solution)/shard_map/ppermute | solution.py:23
  43.4 14.6 %collective-permute-start.4 = (f32[96,832]{1,0:T(8,128)S(1)}, f32[96,832]{1,0:T(8,128)S(1)}, u32[]{:S(2)}, u32[]{:S(2)}) collective-permute-start(f32[96,832]{1,0:T(8,128)S(1)} %get-tuple-element.11), channel_id=1, source_target_pairs={{0,8},{8,16},{16,24},{1,9},{9,17},{17,25},{2,10},{10,18},{18,26},{... | collective-permute-start | bytes 958472 | tf_op jit(solution)/shard_map/ppermute | solution.py:21
  59.8 7.5 %collective-permute-start.6 = (f32[96,4992]{1,0:T(8,128)}, f32[96,4992]{1,0:T(8,128)S(1)}, u32[]{:S(2)}, u32[]{:S(2)}) collective-permute-start(f32[96,4992]{1,0:T(8,128)} %concatenate.11), channel_id=1, source_target_pairs={{0,1},{1,2},{2,3},{3,4},{4,5},{5,6},{6,7},{8,9},{9,10},{10,11},{11... | collective-permute-start | bytes 5750792 | tf_op jit(solution)/shard_map/ppermute | solution.py:33
  67.2 26.9 %collective-permute-start.7 = (f32[96,4992]{1,0:T(8,128)S(1)}, f32[96,4992]{1,0:T(8,128)S(1)}, u32[]{:S(2)}, u32[]{:S(2)}) collective-permute-start(f32[96,4992]{1,0:T(8,128)S(1)} %collective-permute-done.6), channel_id=1, source_target_pairs={{0,1},{1,2},{2,3},{3,4},{4,5},{5,6},{6,7},{8,9},{9,10},{10,11},{11... | collective-permute-start | bytes 5750792 | tf_op jit(solution)/shard_map/ppermute | solution.py:33
  90.8 3.4 copy-start.2
  97.1 1.3 copy-start.3
  134.9 1.4 copy-start.4
  136.2 1.8 copy-start.6
  136.2 1.8 copy-start.7
  136.3 1.8 copy-start.8
  348.8 8.7 %copy-start.1 = (f32[96,81]{0,1:T(8,128)S(1)}, f32[96,81]{0,1:T(8,128)}, u32[]{:S(2)}) copy-start(f32[96,81]{0,1:T(8,128)} %param.15) | copy-start | bytes 93316
where the time goes:
time: 364 us; the launch traced here: 358 us
  other arithmetic  131 us (36%)
  local copies, waits for them, and re-layouts  71.1 us (20%)
  starting transfers between devices  52.7 us (14%)
  matrix products  43.6 us (12%)
  blocking collectives  33 us (9%)
  waiting for transfers between devices  25.4 us (7%)
    unnamed x1, other arithmetic  120 us
    unnamed x21, local copies, waits for them, and re-layouts  40.4 us
    dot_general x27, matrix products, middle_conv(): jnp.dot(tap_weights[step_time * 9 + step_row * 3 + step_col], tap_slab, p...  39.3 us
    ppermute x4, starting transfers between devices, passed_along(): return lax.ppermute(block, axis, route)  33.4 us
    all_to_all x1, blocking collectives, body(): lax.all_to_all(patches, 'seq', split_axis=2, concat_axis=0, tiled=True)  33 us
    reshape x1, local copies, waits for them, and re-layouts, body(): patches = patches.reshape(1, rows_dev // 2, row_len // 2 * latent_chans * 4)  15.5 us
    ppermute x2, waiting for transfers between devices, extended(): lax.ppermute(tail, axis, [(i, (i + 1) % count) for i in range(ends)])  11.1 us
    all_to_all x1, local copies, waits for them, and re-layouts, body(): lax.all_to_all(patches, 'seq', split_axis=2, concat_axis=0, tiled=True)  8.7 us
  transfers between devices with their start and end apart: 10, of which 8 were waited for; matrix products, arithmetic and copies ran while one was open for 2% of the time, Pallas kernels for 0%

commit v1 on v0

v1 whole, which is shorter than its diff:
```python
import functools

import jax
import jax.numpy as jnp
from jax import lax
from jax.experimental import pallas as pl
from jax.experimental.pallas import tpu as pltpu
from jax.sharding import PartitionSpec as P

FRAMES = 4
EPSILON = 1e-06
LANES = 128
TILES = 6
MOVED = 64
SLOT = 80
BF16 = jnp.bfloat16
F32 = jnp.float32
F8 = jnp.float8_e4m3fn
NT = (((1,), (1,)), ((), ()))
TN = (((0,), (0,)), ((), ()))


def iota(shape, dim):
    return lax.broadcasted_iota(jnp.int32, shape, dim)


def halves(values):
    high = values.astype(BF16)
    return high, (values - high.astype(F32)).astype(BF16)


def mm(a, b):
    return jnp.dot(a, b, preferred_element_type=F32)


def mm_tn(a, b):
    return lax.dot_general(a, b, TN, preferred_element_type=F32)


def send_kernel(groups_dp, groups_seq, row_len, loaded_any, tiles_any, out_ref, loaded_ref, tiles_ref, sems):
    copies = [
        pltpu.make_async_copy(loaded_any, loaded_ref, sems.at[0]),
        pltpu.make_async_copy(tiles_any, tiles_ref, sems.at[1]),
    ]
    for copy in copies:
        copy.start()
    for copy in copies:
        copy.wait()
    wide = row_len // groups_seq
    step = 2 * row_len // LANES
    frame = lax.axis_index("seq")
    lane = iota((TILES, LANES), 1)
    which = iota((TILES, LANES), 0)
    label = jnp.zeros((TILES, LANES), F32)
    for tile in range(TILES):
        label = jnp.where(which == tile, tiles_ref[0, tile].astype(F32), label)
    for s in range(groups_seq):
        windows = []
        for r in range(2):
            block, off = divmod(r * row_len + wide * s - 2, LANES)
            first = jnp.zeros((TILES, LANES), F32)
            second = first
            if block >= 0:
                first = loaded_ref[:, 0, block * LANES : (block + 1) * LANES]
            if block + 1 < step:
                second = loaded_ref[:, 0, (block + 1) * LANES : (block + 2) * LANES]
            window = jnp.where(lane >= off, first, second)
            if off:
                window = pltpu.roll(window, LANES - off, 1)
            column = lane + (wide * s - 2)
            inside = (column >= 0) & (column < row_len) & (lane < wide + 4)
            window = jnp.where(inside, window, 0.0)
            window = jnp.where(lane == wide + 4, label, window)
            place = (2 * frame + r).astype(F32)
            windows.append(jnp.where(lane == wide + 5, place, window))
        for j in range(3):
            rows = [window[t : t + 1] for window in windows for t in (j, j + 3)]
            rows = jnp.concatenate(rows, 0)
            for i in range(groups_dp):
                out_ref[i * groups_seq + s, :, j * LANES : (j + 1) * LANES] = rows


def prep_kernel(
    clips, wide, bucket_ref, in_weight_ref, in_bias_ref, bucket_bias_ref, norm_gain_ref, mid_weight_ref, mid_bias_ref,
    head_gain_ref, head_weight_ref, head_bias_ref, entry_ref, mid_ref, mend_ref, head_ref, cols_ref, fold_ref,
):
    ch = norm_gain_ref.shape[1]
    zch = head_bias_ref.shape[1]
    lane_pad = jnp.zeros((1, LANES - ch), F32)
    rows = [0.5 * norm_gain_ref[...], mid_bias_ref[...], 0.5 * head_gain_ref[...]]
    for clip in range(clips):
        rows.append(in_bias_ref[...] + bucket_bias_ref[pl.ds(bucket_ref[clip], 1), :])
    rows = [jnp.concatenate([row, lane_pad], 1) for row in rows]
    rows.append(jnp.zeros((LANES - len(rows), LANES), F32))
    table = jnp.concatenate(rows, 0).T
    for n in range(3):
        cols_ref[n] = jnp.broadcast_to(table[:ch, n : n + 1], (ch, LANES))
    spots = iota((ch, 2 * LANES), 1)
    offsets = jnp.zeros((ch, 2 * LANES), F32)
    for clip in range(clips):
        offsets = jnp.where(spots == 72 + clip, table[:ch, 3 + clip : 4 + clip], offsets)

    w_high, w_low = halves(in_weight_ref[...])
    taps = in_weight_ref.shape[0]
    tap = iota((taps, 2 * LANES), 0)
    place = iota((taps, 2 * LANES), 1)
    back = jnp.where(place >= SLOT, 1, 0) + jnp.where(place >= 2 * SLOT, 1, 0)
    inner = place - back * SLOT
    step_col = jnp.where(inner >= 24, 1, 0) + jnp.where(inner >= 48, 1, 0)
    colour = (inner - 24 * step_col) >> 3
    frame_row = inner & 7
    used = (place < 3 * SLOT) & (inner < 72)
    for h in range(6):
        step_row = frame_row - h
        wanted = 27 * (2 - back) + 9 * step_row + 3 * step_col + colour
        hot = used & (step_row >= 0) & (step_row < 3) & (tap == wanted)
        hot = jnp.where(hot, 1.0, 0.0).astype(BF16)
        off_high, off_low = halves(offsets)
        high = (mm_tn(w_high, hot) + off_high.astype(F32)).astype(BF16)
        low = (mm_tn(w_low, hot) + off_low.astype(F32)).astype(BF16)
        entry_ref[h * ch : (h + 1) * ch, :] = jnp.concatenate([high, low, high], 1)

    for d in range(3):
        blocks, mends = [], []
        for back in range(3):
            taps = [mid_weight_ref[9 * (2 - back) + 3 * b + d] for b in range(3)]
            exact = jnp.concatenate(taps, 1)
            high = exact.astype(BF16)
            blocks += [high, high[:, :MOVED]]
            mends += [(exact - high.astype(F32)) * 2.0**20, exact[:, MOVED:] * 2.0**11]
        for ref, parts, dtype in ((mid_ref, blocks, BF16), (mend_ref, mends, F8)):
            depth = sum(part.shape[1] for part in parts)
            if depth < ref.shape[1]:
                parts.append(jnp.zeros((ch, ref.shape[1] - depth), parts[0].dtype))
            ref[d * ch : (d + 1) * ch, :] = jnp.concatenate(parts, 1).astype(dtype)

    row = iota((LANES, zch), 0)
    channel = (row >> 2) & (zch - 1)
    pick = jnp.where(channel == iota((LANES, zch), 1), 1.0, 0.0)
    high, low = halves(head_weight_ref[...])
    parity = (iota((LANES, ch), 0) >> 1) & 1
    parts = []
    for weight in (high, low):
        spread = mm(pick.astype(BF16), weight)
        parts.append(jnp.concatenate([jnp.where(parity == r, spread, 0.0) for r in range(2)], 1))
    bias = jnp.sum(pick * head_bias_ref[...], axis=1, keepdims=True)
    bias_high, bias_low = halves(jnp.broadcast_to(bias, (LANES, 64)))
    spot = iota((LANES, 64), 1)
    tail = jnp.where(spot == 0, bias_high.astype(F32), jnp.where(spot == 1, bias_low.astype(F32), 0.0))
    head_ref[...] = jnp.concatenate([parts[0], parts[1], parts[0], tail], 1).astype(BF16)

    out = iota(fold_ref.shape, 0)
    src = iota(fold_ref.shape, 1)
    lane = src & (LANES - 1)
    hit = (((src >> 7) & 1) == (out & 1)) & (lane >= 2) & (lane < wide + 2) & (((lane - 2) >> 2) == (out >> 1))
    fold_ref[...] = jnp.where(hit, 1.0, 0.0).astype(BF16)


def main_kernel(
    clips, groups_dp, row_len, recv_ref, entry_ref, mid_ref, mend_ref, head_ref, cols_ref, fold_ref, out_any,
    pixels, q_high, q_low, s_high, s_mend, kept, tokens_ref, sems,
):
    frames_all = clips * FRAMES
    wide = out_any.shape[2] // 32
    ch = kept.shape[1]
    deep, deep_mend = 3 * ch + MOVED, 6 * ch - MOVED
    band = lax.axis_index("dp")
    column_band = lax.axis_index("seq")

    cells = [recv_ref[:, k, j * LANES : (j + 1) * LANES] for k in range(4) for j in range(3)]
    high, low = halves(jnp.concatenate(cells, 0))
    picks = iota((16, LANES), 0)
    picks = iota((16, LANES), 1) == jnp.where(picks < 8, wide + 4, wide + 5)
    tags = lax.dot_general(jnp.where(picks, 1.0, 0.0).astype(BF16), high, NT, preferred_element_type=F32)
    label, place = tags[:8], tags[8:]
    row = iota(label.shape, 0)
    pair = (band * 4 - 2 + row) >> 1
    first = ((pair >> 1) * TILES + (pair & 1)).astype(F32)
    of_colour = [label == first + 2.0 * c for c in range(3)]
    blocks = []
    for g in range(frames_all):
        here = place == (2 * g + (row & 1)).astype(F32)
        blocks += [jnp.where(here & hit, 1.0, 0.0) for hit in of_colour]
    order = jnp.concatenate(blocks, 0).astype(BF16)
    pixels[...] = mm(order, jnp.concatenate([high, low], 1))

    early = pl.ds(FRAMES * SLOT, q_high.shape[1] - FRAMES * SLOT)
    for ref in (q_high, q_low):
        for n in range(ref.shape[0]):
            ref[n, early, :] = jnp.zeros((early.size, LANES), BF16)

    lane = iota((1, LANES), 1)
    column = lane + (wide * column_band - 2)
    inside = jnp.where((column >= 0) & (column < row_len), 1.0, 0.0)
    masks = [inside] * 6
    masks[0] = jnp.where(band > 0, inside, 0.0)
    masks[5] = jnp.where(band < groups_dp - 1, inside, 0.0)
    ones = jnp.where(iota((64, 2 * LANES), 0) < 2, 1.0, 0.0).astype(BF16)
    phase = iota((LANES, 2 * LANES), 0)
    phase = ((phase >> 6) << 1) + (phase & 1)
    on_phase = ((iota((LANES, 2 * LANES), 1) - 2) & 3) == phase

    def active(values, half_gain, mask):
        square = jnp.sum(values * values, axis=0, keepdims=True) * (1.0 / ch)
        scale = lax.rsqrt(square + EPSILON)
        if mask is not None:
            scale = scale * mask
        half = values * scale * half_gain
        return half + half * jnp.tanh(half)

    def gather(clip):
        side = clip % 2
        for f in range(FRAMES):
            rows = pixels[(clip * FRAMES + f) * 24 : (clip * FRAMES + f + 1) * 24, :]
            for part, ref in ((0, q_high), (1, q_low)):
                cells = rows[:, part * LANES : (part + 1) * LANES]
                spare = jnp.where(iota((8, LANES), 0) == (-1 if part else clip), 1.0, 0.0)
                stack = [pltpu.roll(cells, 1, 1), cells, pltpu.roll(cells, LANES - 1, 1), spare]
                ref[side, (FRAMES - 1 - f) * SLOT : (FRAMES - f) * SLOT, :] = jnp.concatenate(stack, 0).astype(BF16)

    def enter(clip, f):
        side = clip % 2
        at = [(FRAMES - 1 - f - k) * SLOT for k in range(2)]
        right = [jnp.concatenate([ref[side, p : p + 2 * LANES, :] for p in at], 1) for ref in (q_high, q_low)]
        entry = mm(entry_ref[...], jnp.concatenate([right[0], right[0], right[1]], 0))
        for k in range(2):
            base = FRAMES - 1 - f - k
            for h in range(6):
                cell = entry[h * ch : (h + 1) * ch, k * LANES : (k + 1) * LANES]
                if 1 <= h <= 4:
                    kept[side * FRAMES + f + k, :, (h - 1) * LANES : h * LANES] = cell + cols_ref[1]
                act = active(cell, cols_ref[0], masks[h])
                act_high = act.astype(BF16)
                rest = act - act_high.astype(F32)
                low = rest[:MOVED].astype(BF16)
                rest = (rest * 2.0**13).astype(F8)
                coarse = (act * 2.0**4).astype(F8)
                for b in range(3):
                    if 0 <= h - b < 4:
                        lanes = pl.ds((h - b) * LANES, LANES)
                        at = base * deep + b * ch
                        s_high[side, at : at + ch, lanes] = act_high
                        at = base * deep_mend + b * ch
                        s_mend[side, at : at + ch, lanes] = coarse
                        at += 3 * ch - MOVED
                        if b:
                            s_mend[side, at : at + ch, lanes] = rest
                        else:
                            s_mend[side, at + MOVED : at + ch, lanes] = rest[MOVED:]
                            at = base * deep + 3 * ch
                            s_high[side, at : at + MOVED, lanes] = low

    def finish(clip, f):
        side = clip % 2
        def conv(weights, stack, per_frame):
            depth = per_frame * min(f + 1, 3)
            start = (FRAMES - 1 - f) * per_frame
            right = stack[side, start : start + depth, :]
            if depth % LANES:
                right = jnp.concatenate([right, jnp.zeros((-depth % LANES, 4 * LANES), stack.dtype)], 0)
            return mm(weights[:, : right.shape[0]], right)

        total = conv(mid_ref, s_high, deep) + conv(mend_ref, s_mend, deep_mend) * 2.0**-24
        acts = []
        for h in range(4):
            cell = total[:, h * LANES : (h + 1) * LANES]
            mixed = kept[side * FRAMES + f, :, h * LANES : (h + 1) * LANES] + cell[ch : 2 * ch]
            mixed = mixed + pltpu.roll(cell[:ch], 1, 1) + pltpu.roll(cell[2 * ch :], LANES - 1, 1)
            acts.append(active(mixed, cols_ref[2], None))
        top = jnp.concatenate([acts[0], acts[2]], 1)
        bottom = jnp.concatenate([acts[1], acts[3]], 1)
        act_high, act_low = halves(jnp.concatenate([top, bottom], 0))
        latent = mm(head_ref[...], jnp.concatenate([act_high, act_high, act_low, ones], 0))
        lat_high, lat_low = halves(jnp.where(on_phase, latent, 0.0))
        tokens = lax.dot_general(
            fold_ref[...], jnp.concatenate([lat_high, lat_low], 1), NT, preferred_element_type=F32
        )
        g = clip * FRAMES + f
        for n in range(wide // 4):
            tokens_ref[g, :, n * LANES : (n + 1) * LANES] = tokens[2 * n : 2 * n + 2]
        pltpu.make_async_copy(tokens_ref.at[g], out_any.at[g], sems.at[g]).start()

    gather(0)
    enter(0, 0)
    enter(0, 2)
    for clip in range(clips):
        later = clip + 1 < clips
        finish(clip, 0)
        if later:
            gather(clip + 1)
            enter(clip + 1, 0)
        finish(clip, 1)
        finish(clip, 2)
        if later:
            enter(clip + 1, 2)
        finish(clip, 3)
    for g in range(frames_all):
        pltpu.make_async_copy(tokens_ref.at[g], out_any.at[g], sems.at[g]).wait()


def body(
    loaded, tile_rows, bucket_ids, in_weight, in_bias, bucket_bias, norm_gain, mid_weight, mid_bias, head_gain,
    head_weight, head_bias,
):
    groups_dp = lax.axis_size("dp")
    groups_seq = lax.axis_size("seq")
    row_len = loaded.shape[2] // 2
    wide = row_len // groups_seq
    clips = bucket_ids.shape[0]
    frames_all = clips * FRAMES
    ch = norm_gain.shape[0]
    devices = groups_dp * groups_seq
    deep, deep_mend = 3 * ch + MOVED, 6 * ch - MOVED
    vmem = pl.BlockSpec(memory_space=pltpu.VMEM)
    place = pl.BlockSpec(memory_space=pl.ANY)
    part = pltpu.CompilerParams(vmem_limit_bytes=40 * 1024 * 1024)
    whole = pltpu.CompilerParams(vmem_limit_bytes=60 * 1024 * 1024)

    message = pl.pallas_call(
        functools.partial(send_kernel, groups_dp, groups_seq, row_len),
        out_shape=jax.ShapeDtypeStruct((devices, 4, 3 * LANES), F32),
        in_specs=[place] * 2,
        out_specs=vmem,
        scratch_shapes=[
            pltpu.VMEM((TILES, 1, 2 * row_len), F32),
            pltpu.SMEM((1, TILES), jnp.int32),
            pltpu.SemaphoreType.DMA((2,)),
        ],
        compiler_params=whole,
        name="send_windows",
    )(loaded.transpose(1, 0, 2), tile_rows)
    arrived = lax.all_to_all(message, ("dp", "seq"), split_axis=0, concat_axis=0, tiled=True)

    fold_rows = -(-(wide // 2) // 16) * 16
    operands = (
        bucket_ids, in_weight.T, in_bias[None], bucket_bias, norm_gain[None], mid_weight, mid_bias[None],
        head_gain[None], head_weight, head_bias[None],
    )
    weights = pl.pallas_call(
        functools.partial(prep_kernel, clips, wide),
        out_shape=(
            jax.ShapeDtypeStruct((6 * ch, 6 * LANES), BF16),
            jax.ShapeDtypeStruct((3 * ch, -(-3 * deep // LANES) * LANES), BF16),
            jax.ShapeDtypeStruct((3 * ch, -(-3 * deep_mend // LANES) * LANES), F8),
            jax.ShapeDtypeStruct((LANES, 6 * ch + 64), BF16),
            jax.ShapeDtypeStruct((3, ch, LANES), F32),
            jax.ShapeDtypeStruct((fold_rows, 4 * LANES), BF16),
        ),
        in_specs=[pl.BlockSpec(memory_space=pltpu.SMEM)] + [vmem] * (len(operands) - 1),
        out_specs=(vmem,) * 6,
        compiler_params=part,
        name="prepare_weights",
    )(*operands)
    sides = min(clips, 2)
    return pl.pallas_call(
        functools.partial(main_kernel, clips, groups_dp, row_len),
        out_shape=jax.ShapeDtypeStruct((frames_all, 2, wide * 32), F32),
        in_specs=[vmem] * 7,
        out_specs=place,
        scratch_shapes=[
            pltpu.VMEM((frames_all * 24, 2 * LANES), F32),
            pltpu.VMEM((sides, (FRAMES + 2) * SLOT + 16, LANES), BF16),
            pltpu.VMEM((sides, (FRAMES + 2) * SLOT + 16, LANES), BF16),
            pltpu.VMEM((sides, FRAMES * deep, 4 * LANES), BF16),
            pltpu.VMEM((sides, FRAMES * deep_mend, 4 * LANES), F8),
            pltpu.VMEM((sides * FRAMES, ch, 4 * LANES), F32),
            pltpu.VMEM((frames_all, 2, wide * 32), F32),
            pltpu.SemaphoreType.DMA((frames_all,)),
        ],
        compiler_params=part,
        name="encode_columns",
    )(arrived, *weights)


def solution(mesh):
    return jax.shard_map(
        body,
        mesh=mesh,
        in_specs=(P("seq", "dp", None), P("seq", "dp")) + (P(),) * 10,
        out_specs=P(None, "dp", "seq"),
        check_vma=False,
    )
```

time: 364 us -> 29.3 us (0.08)
  the two profiles are of different devices: /device:TPU:6 before, /device:TPU:1 now
where the time goes in v1:
time: 29.3 us; the launch traced here: 28.7 us
  Pallas kernels  14 us (48%)
  local copies, waits for them, and re-layouts  7.41 us (25%)
  starting transfers between devices  7.1 us (24%)
    pallas_call x1, Pallas kernels, body(): pl.pallas_call(functools.partial(main_kernel, clips, groups_dp, row_len),...  10.7 us
    unnamed x20, local copies, waits for them, and re-layouts  7.41 us
    all_to_all x1, starting transfers between devices, body(): lax.all_to_all(message, ('dp', 'seq'), split_axis=0, concat_axis=0, tiled...  7.1 us
    pallas_call x1, Pallas kernels, body(): pl.pallas_call(functools.partial(prep_kernel, clips, wide), out_shape=(ja...  1.78 us
    pallas_call x1, Pallas kernels, body(): pl.pallas_call(functools.partial(send_kernel, groups_dp, groups_seq, row_...  1.6 us
  transfers between devices with their start and end apart: 1, of which 1 were waited for; matrix products, arithmetic and copies ran while one was open for 0% of the time, Pallas kernels for 6%

profile of v1, /device:TPU:1, one launch (start us, length us, event | category | flops | bytes accessed | tf_op | source)
XLA Modules:
  0.0 28.7 jit_solution(11762839912839685989)
XLA Ops:
  0.0 1.6 %send_windows.1 = f32[32,4,384]{2,1,0:T(4,128)} custom-call(f32[6,1,1664]{2,1,0:T(1,128)} %bitcast.13, s32[1,6]{1,0:T(1,128)} %tiles_any.1), custom_call_target="tpu_custom_call" | custom-call | tf_op jit(solution)/shard_map/send_windows/pallas_call | solution.py:319
  1.6 7.1 %all-to-all-start = ((f32[32,4,384]{2,1,0:T(4,128)}), f32[32,4,384]{2,1,0:T(4,128)S(1)}, u32[]{:S(2)}, u32[]{:S(2)}) async-start(f32[32,4,384]{2,1,0:T(4,128)} %send_windows.1), calls=%async_computation | async-start | bytes 393216 | tf_op jit(solution)/shard_map/all_to_all | solution.py:332
  8.7 0.0 copy-start
  8.7 1.3 %copy-done = f32[27,96,96]{2,1,0:T(8,128)S(1)} copy-done((f32[27,96,96]{2,1,0:T(8,128)S(1)}, f32[27,96,96]{2,1,0:T(8,128)}, u32[]{:S(2)}) %copy-start) | copy-done | bytes 995352
  10.0 0.0 copy-start.1
  10.0 0.8 %copy-done.1 = f32[96,81]{0,1:T(8,128)S(1)} copy-done((f32[96,81]{0,1:T(8,128)S(1)}, f32[96,81]{0,1:T(8,128)}, u32[]{:S(2)}) %copy-start.1) | copy-done | bytes 31128
  10.8 0.0 copy-start.2
  10.8 0.7 %copy-done.2 = f32[16,96]{1,0:T(8,128)S(1)} copy-done((f32[16,96]{1,0:T(8,128)S(1)}, f32[16,96]{1,0:T(8,128)}, u32[]{:S(2)}) %copy-start.2) | copy-done | bytes 6168
  11.5 0.0 copy-start.3
  11.5 0.7 %copy-done.3 = f32[4,96]{1,0:T(4,128)S(1)} copy-done((f32[4,96]{1,0:T(4,128)S(1)}, f32[4,96]{1,0:T(4,128)}, u32[]{:S(2)}) %copy-start.3) | copy-done | bytes 1560
  12.2 0.0 copy-start.4
  12.2 0.7 %copy-done.4 = s32[2]{0:T(128)S(1)} copy-done((s32[2]{0:T(128)S(1)}, s32[2]{0:T(128)}, u32[]{:S(2)}) %copy-start.4) | copy-done | bytes 32
  12.9 0.0 copy-start.5
  12.9 0.7 %copy-done.5 = f32[96]{0:T(128)S(1)} copy-done((f32[96]{0:T(128)S(1)}, f32[96]{0:T(128)}, u32[]{:S(2)}) %copy-start.5) | copy-done | bytes 408
  13.5 0.0 copy-start.6
  13.5 0.7 %copy-done.6 = f32[96]{0:T(128)S(1)} copy-done((f32[96]{0:T(128)S(1)}, f32[96]{0:T(128)}, u32[]{:S(2)}) %copy-start.6) | copy-done | bytes 408
  14.2 0.0 copy-start.7
  14.2 0.7 %copy-done.7 = f32[96]{0:T(128)S(1)} copy-done((f32[96]{0:T(128)S(1)}, f32[96]{0:T(128)}, u32[]{:S(2)}) %copy-start.7) | copy-done | bytes 408
  14.8 0.0 copy-start.8
  14.8 0.7 %copy-done.8 = f32[96]{0:T(128)S(1)} copy-done((f32[96]{0:T(128)S(1)}, f32[96]{0:T(128)}, u32[]{:S(2)}) %copy-start.8) | copy-done | bytes 408
  15.5 0.0 copy-start.9
  15.5 0.7 %copy-done.9 = f32[16]{0:T(128)S(1)} copy-done((f32[16]{0:T(128)S(1)}, f32[16]{0:T(128)}, u32[]{:S(2)}) %copy-start.9) | copy-done | bytes 88
  16.1 1.8 %prepare_weights.1 = (bf16[576,768]{1,0:T(8,128)(2,1)S(1)}, bf16[288,1152]{1,0:T(8,128)(2,1)S(1)}, f8e4m3fn[288,1536]{1,0:T(32,128)(4,1)S(1)}, bf16[128,640]{1,0...) custom-call(s32[2]{0:T(128)S(1)} %copy-done.4, f32[81,96]{1,0:T(8,128)S(1)} %bitcast.7, ...), custom_call_target="tpu_custom_call" | custom-call | tf_op jit(solution)/shard_map/prepare_weights/pallas_call | solution.py:339
  17.9 0.1 all-to-all-done.recv_ref
  18.0 10.7 %encode_columns.1 = f32[8,2,3328]{2,1,0:T(2,128)} custom-call(f32[32,4,384]{2,1,0:T(4,128)S(1)} %all-to-all-done.recv_ref, bf16[576,768]{1,0:T(8,128)(2,1)S(1)} %get-tuple-element.11.entry_ref, bf16[288,1152]{1,0:T(8,128)(2,1)S(1)} %get-tuple-element.12.mid_ref, f8e4m3fn[288,1536]{1,0:T(32,128)(4,1)S(1)} %get-tuple-element.13.mend_ref, ...), custom_call_target="tpu_custom_call" | custom-call | tf_op jit(solution)/shard_map/encode_columns/pallas_call | solution.py:355
Async XLA Ops:
  1.6 16.4 %all-to-all-start = ((f32[32,4,384]{2,1,0:T(4,128)}), f32[32,4,384]{2,1,0:T(4,128)S(1)}, u32[]{:S(2)}, u32[]{:S(2)}) async-start(f32[32,4,384]{2,1,0:T(4,128)} %send_windows.1), calls=%async_computation | async-start | bytes 393216 | tf_op jit(solution)/shard_map/all_to_all | solution.py:332
  8.7 1.3 %copy-start = (f32[27,96,96]{2,1,0:T(8,128)S(1)}, f32[27,96,96]{2,1,0:T(8,128)}, u32[]{:S(2)}) copy-start(f32[27,96,96]{2,1,0:T(8,128)} %mid_weight_ref.1) | copy-start | bytes 2985988
  10.0 0.8 %copy-start.1 = (f32[96,81]{0,1:T(8,128)S(1)}, f32[96,81]{0,1:T(8,128)}, u32[]{:S(2)}) copy-start(f32[96,81]{0,1:T(8,128)} %param.15) | copy-start | bytes 93316
  10.8 0.7 %copy-start.2 = (f32[16,96]{1,0:T(8,128)S(1)}, f32[16,96]{1,0:T(8,128)}, u32[]{:S(2)}) copy-start(f32[16,96]{1,0:T(8,128)} %head_weight_ref.1) | copy-start | bytes 18436
  11.5 0.7 %copy-start.3 = (f32[4,96]{1,0:T(4,128)S(1)}, f32[4,96]{1,0:T(4,128)}, u32[]{:S(2)}) copy-start(f32[4,96]{1,0:T(4,128)} %bucket_bias_ref.1) | copy-start | bytes 4612
  12.2 0.7 %copy-start.4 = (s32[2]{0:T(128)S(1)}, s32[2]{0:T(128)}, u32[]{:S(2)}) copy-start(s32[2]{0:T(128)} %bucket_ref.1) | copy-start | bytes 28
  12.9 0.7 %copy-start.5 = (f32[96]{0:T(128)S(1)}, f32[96]{0:T(128)}, u32[]{:S(2)}) copy-start(f32[96]{0:T(128)} %param.16) | copy-start | bytes 1156
  13.5 0.7 %copy-start.6 = (f32[96]{0:T(128)S(1)}, f32[96]{0:T(128)}, u32[]{:S(2)}) copy-start(f32[96]{0:T(128)} %param.18) | copy-start | bytes 1156
  14.2 0.7 %copy-start.7 = (f32[96]{0:T(128)S(1)}, f32[96]{0:T(128)}, u32[]{:S(2)}) copy-start(f32[96]{0:T(128)} %param.20) | copy-start | bytes 1156
  14.8 0.7 %copy-start.8 = (f32[96]{0:T(128)S(1)}, f32[96]{0:T(128)}, u32[]{:S(2)}) copy-start(f32[96]{0:T(128)} %param.21) | copy-start | bytes 1156
  15.5 0.7 %copy-start.9 = (f32[16]{0:T(128)S(1)}, f32[16]{0:T(128)}, u32[]{:S(2)}) copy-start(f32[16]{0:T(128)} %param.23) | copy-start | bytes 196

commit v2 on v1

v2 whole, which is shorter than its diff:
```python
import functools

import jax
import jax.numpy as jnp
from jax import lax
from jax.experimental import pallas as pl
from jax.experimental.pallas import tpu as pltpu
from jax.sharding import PartitionSpec as P

FRAMES = 4
EPSILON = 1e-06
LANES = 128
TILES = 6
SLOT = 48
BAND = 3 * SLOT
BF16 = jnp.bfloat16
F32 = jnp.float32
F8 = jnp.float8_e4m3fn
NT = (((1,), (1,)), ((), ()))
TN = (((0,), (0,)), ((), ()))


def iota(shape, dim):
    return lax.broadcasted_iota(jnp.int32, shape, dim)


def halves(values):
    high = values.astype(BF16)
    return high, (values - high.astype(F32)).astype(BF16)


def mm(a, b):
    return jnp.dot(a, b, preferred_element_type=F32)


def mm_tn(a, b):
    return lax.dot_general(a, b, TN, preferred_element_type=F32)


def split_row(row):
    frame_row = sum(jnp.where(row >= 3 * n, 1, 0) for n in range(1, 8))
    return frame_row, row - 3 * frame_row


def send_kernel(groups_dp, groups_seq, row_len, loaded_any, tiles_any, out_ref, loaded_ref, tiles_ref, sems):
    copies = [
        pltpu.make_async_copy(loaded_any, loaded_ref, sems.at[0]),
        pltpu.make_async_copy(tiles_any, tiles_ref, sems.at[1]),
    ]
    for copy in copies:
        copy.start()
    for copy in copies:
        copy.wait()
    wide = row_len // groups_seq
    step = 2 * row_len // LANES
    frame = lax.axis_index("seq")
    lane = iota((TILES, LANES), 1)
    which = iota((TILES, LANES), 0)
    label = jnp.zeros((TILES, LANES), F32)
    for tile in range(TILES):
        label = jnp.where(which == tile, tiles_ref[0, tile].astype(F32), label)
    for s in range(groups_seq):
        windows = []
        for r in range(2):
            block, off = divmod(r * row_len + wide * s - 2, LANES)
            first = jnp.zeros((TILES, LANES), F32)
            second = first
            if block >= 0:
                first = loaded_ref[:, 0, block * LANES : (block + 1) * LANES]
            if block + 1 < step:
                second = loaded_ref[:, 0, (block + 1) * LANES : (block + 2) * LANES]
            window = jnp.where(lane >= off, first, second)
            if off:
                window = pltpu.roll(window, LANES - off, 1)
            column = lane + (wide * s - 2)
            inside = (column >= 0) & (column < row_len) & (lane < wide + 4)
            window = jnp.where(inside, window, 0.0)
            window = jnp.where(lane == wide + 4, label, window)
            place = (2 * frame + r).astype(F32)
            windows.append(jnp.where(lane == wide + 5, place, window))
        for j in range(3):
            rows = [window[t : t + 1] for window in windows for t in (j, j + 3)]
            rows = jnp.concatenate(rows, 0)
            for i in range(groups_dp):
                out_ref[i * groups_seq + s, :, j * LANES : (j + 1) * LANES] = rows


def collect_kernel(clips, *refs):
    sources, out_ref, held, sems = refs[:8], refs[8], refs[9:17], refs[17]
    copies = [pltpu.make_async_copy(src, dst, sems.at[n]) for n, (src, dst) in enumerate(zip(sources, held))]
    for copy in copies:
        copy.start()
    out_ref[...] = jnp.zeros(out_ref.shape, F32)
    for copy in copies:
        copy.wait()
    bucket, in_bias, bucket_bias, norm_gain, mid_bias, head_gain, head_weight, head_bias = held
    ch = norm_gain.shape[1]
    out_ref[0:1, :ch] = 0.5 * norm_gain[...]
    out_ref[1:2, :ch] = mid_bias[...]
    out_ref[2:3, :ch] = 0.5 * head_gain[...]
    for clip in range(clips):
        out_ref[3 + clip : 4 + clip, :ch] = in_bias[...] + bucket_bias[pl.ds(bucket[clip], 1), :]
    out_ref[8:9, : head_bias.shape[1]] = head_bias[...]
    out_ref[16:, :ch] = head_weight[...]


def prep_kernel(
    clips, wide, vectors_ref, in_weight_ref, mid_weight_ref, entry_ref, mid_ref, mend_ref, head_ref, cols_ref, fold_ref
):
    ch = cols_ref.shape[1]
    zch = vectors_ref.shape[0] - 16
    rows = [vectors_ref[...], jnp.zeros((LANES - vectors_ref.shape[0], LANES), F32)]
    table = jnp.concatenate(rows, 0).T
    for n in range(3):
        cols_ref[n] = jnp.broadcast_to(table[:ch, n : n + 1], (ch, LANES))
    spots = iota((ch, 4 * LANES - 3 * BAND), 1)
    offsets = jnp.zeros(spots.shape, F32)
    for clip in range(clips):
        exact = jnp.broadcast_to(table[:ch, 3 + clip : 4 + clip], spots.shape)
        off_high, off_low = halves(exact)
        offsets = jnp.where(spots == 2 * clip, off_high.astype(F32), offsets)
        offsets = jnp.where(spots == 2 * clip + 1, off_low.astype(F32), offsets)
    offsets = offsets.astype(BF16)

    w_high, w_low = halves(in_weight_ref[...])
    taps = in_weight_ref.shape[0]
    tap = iota((taps, 2 * LANES), 0)
    place = iota((taps, 2 * LANES), 1)
    back = jnp.where(place >= SLOT, 1, 0) + jnp.where(place >= 2 * SLOT, 1, 0)
    step_col = ((place - back * SLOT) >> 4) & 3
    for group in range(2):
        frame_row, colour = split_row((place & 15) + 8 * group)
        for k in range(3):
            step_row = frame_row - (3 * group + k)
            wanted = 27 * (2 - back) + 9 * step_row + 3 * step_col + colour
            hot = (place < BAND) & (step_row >= 0) & (step_row < 3) & (tap == wanted)
            hot = jnp.where(hot, 1.0, 0.0).astype(BF16)
            high = mm_tn(w_high, hot).astype(BF16)[:, :BAND]
            low = mm_tn(w_low, hot).astype(BF16)[:, :BAND]
            entry_ref[group, k * ch : (k + 1) * ch, :] = jnp.concatenate([high, low, high, offsets], 1)

    for d in range(3):
        blocks, mends = [], []
        for back in range(3):
            taps = [mid_weight_ref[9 * (2 - back) + 3 * b + d] for b in range(3)]
            exact = jnp.concatenate(taps, 1)
            high = exact.astype(BF16)
            blocks.append(high)
            mends += [(exact - high.astype(F32)) * 2.0**20, exact * 2.0**11]
        for ref, parts, dtype in ((mid_ref, blocks, BF16), (mend_ref, mends, F8)):
            depth = sum(part.shape[1] for part in parts)
            if depth < ref.shape[1]:
                parts.append(jnp.zeros((ch, ref.shape[1] - depth), parts[0].dtype))
            ref[d * ch : (d + 1) * ch, :] = jnp.concatenate(parts, 1).astype(dtype)

    row = iota((LANES, zch), 0)
    channel = (row >> 2) & (zch - 1)
    pick = jnp.where(channel == iota((LANES, zch), 1), 1.0, 0.0)
    high, low = halves(vectors_ref[16:, :ch])
    parity = (iota((LANES, ch), 0) >> 1) & 1
    parts = []
    for weight in (high, low):
        spread = mm(pick.astype(BF16), weight)
        parts.append(jnp.concatenate([jnp.where(parity == r, spread, 0.0) for r in range(2)], 1))
    bias = jnp.sum(pick * vectors_ref[8:9, :zch], axis=1, keepdims=True)
    bias_high, bias_low = halves(jnp.broadcast_to(bias, (LANES, 64)))
    spot = iota((LANES, 64), 1)
    tail = jnp.where(spot == 0, bias_high.astype(F32), jnp.where(spot == 1, bias_low.astype(F32), 0.0))
    head_ref[...] = jnp.concatenate([parts[0], parts[1], parts[0], tail], 1).astype(BF16)

    out = iota(fold_ref.shape, 0)
    src = iota(fold_ref.shape, 1)
    lane = src & (LANES - 1)
    hit = (((src >> 7) & 1) == (out & 1)) & (lane >= 2) & (lane < wide + 2) & (((lane - 2) >> 2) == (out >> 1))
    fold_ref[...] = jnp.where(hit, 1.0, 0.0).astype(BF16)


def main_kernel(
    clips, groups_dp, row_len, recv_ref, entry_ref, mid_ref, mend_ref, head_ref, cols_ref, fold_ref, out_any,
    pixels, q_high, q_low, s_high, s_mend, kept, entered, total, last, tokens_ref, sems,
):
    frames_all = clips * FRAMES
    wide = out_any.shape[2] // 32
    ch = kept.shape[1]
    band = lax.axis_index("dp")
    column_band = lax.axis_index("seq")

    cells = [recv_ref[:, k, j * LANES : (j + 1) * LANES] for k in range(4) for j in range(3)]
    high, low = halves(jnp.concatenate(cells, 0))
    picks = iota((16, LANES), 0)
    picks = iota((16, LANES), 1) == jnp.where(picks < 8, wide + 4, wide + 5)
    tags = lax.dot_general(jnp.where(picks, 1.0, 0.0).astype(BF16), high, NT, preferred_element_type=F32)
    label, place = tags[:8], tags[8:]
    hits, sides = [], []
    for third in range(3):
        frame_row, colour = split_row(iota(label.shape, 0) + 8 * third)
        pair = (band * 4 - 2 + frame_row) >> 1
        hits.append(label == ((pair >> 1) * TILES + (pair & 1) + 2 * colour).astype(F32))
        sides.append((frame_row & 1).astype(F32))
    blocks = []
    for g in range(frames_all):
        for hit, half in zip(hits, sides):
            blocks.append(jnp.where(hit & (place == half + 2.0 * g), 1.0, 0.0))
    order = jnp.concatenate(blocks, 0).astype(BF16)
    pixels[...] = mm(order, jnp.concatenate([high, low], 1))

    for ref in (q_high, q_low):
        for n in range(ref.shape[0]):
            for group in range(2):
                ref[n, group, FRAMES * SLOT :, :] = jnp.zeros((2 * SLOT, LANES), BF16)

    lane = iota((1, LANES), 1)
    column = lane + (wide * column_band - 2)
    inside = jnp.where((column >= 0) & (column < row_len), 1.0, 0.0)
    masks = [inside] * 6
    masks[0] = jnp.where(band > 0, inside, 0.0)
    masks[5] = jnp.where(band < groups_dp - 1, inside, 0.0)
    ones = jnp.where(iota((64, 2 * LANES), 0) < 2, 1.0, 0.0).astype(BF16)
    phase = iota((LANES, 2 * LANES), 0)
    phase = ((phase >> 6) << 1) + (phase & 1)
    on_phase = ((iota((LANES, 2 * LANES), 1) - 2) & 3) == phase

    def active(values, half_gain, mask):
        square = jnp.sum(values * values, axis=0, keepdims=True) * (1.0 / ch)
        scale = lax.rsqrt(square + EPSILON)
        if mask is not None:
            scale = scale * mask
        half = values * scale * half_gain
        return half + half * jnp.tanh(half)

    def gather(clip):
        side = clip % 2
        for f in range(FRAMES):
            rows = pixels[(clip * FRAMES + f) * 24 : (clip * FRAMES + f + 1) * 24, :]
            for part, ref in ((0, q_high), (1, q_low)):
                cells = rows[:, part * LANES : (part + 1) * LANES]
                stack = [pltpu.roll(cells, 1, 1), cells, pltpu.roll(cells, LANES - 1, 1)]
                at = (FRAMES - 1 - f) * SLOT
                for group in range(2):
                    rows_in = jnp.concatenate([step[8 * group : 8 * group + 16] for step in stack], 0)
                    ref[side, group, at : at + SLOT, :] = rows_in.astype(BF16)

    def enter(g, group):
        clip, f = divmod(g, FRAMES)
        at = [(FRAMES - 1 - f - k) * SLOT for k in range(2)]
        high, low = [
            jnp.concatenate([ref[clip % 2, group, p : p + BAND, :] for p in at], 1) for ref in (q_high, q_low)
        ]
        spare = iota((4 * LANES - 3 * BAND, 2 * LANES), 0) >> 1
        spare = jnp.where(spare == clip, 1.0, 0.0).astype(BF16)
        entered[group] = mm(entry_ref[group], jnp.concatenate([high, high, low, spare], 0))

    def activate(g, rows):
        clip, f = divmod(g, FRAMES)
        side, base, k = clip % 2, FRAMES - 1 - f, f % 2
        for h in rows:
            cell = entered[h // 3, h % 3 * ch : (h % 3 + 1) * ch, k * LANES : (k + 1) * LANES]
            if 1 <= h <= 4:
                kept[side * FRAMES + f, :, (h - 1) * LANES : h * LANES] = cell + cols_ref[1]
            act = active(cell, cols_ref[0], masks[h])
            act_high = act.astype(BF16)
            rest = ((act - act_high.astype(F32)) * 2.0**13).astype(F8)
            coarse = (act * 2.0**4).astype(F8)
            for b in range(3):
                if 0 <= h - b < 4:
                    lanes = pl.ds((h - b) * LANES, LANES)
                    s_high[side, pl.ds((3 * base + b) * ch, ch), lanes] = act_high
                    s_mend[side, pl.ds((6 * base + b) * ch, ch), lanes] = coarse
                    s_mend[side, pl.ds((6 * base + 3 + b) * ch, ch), lanes] = rest

    def convolve(g, p):
        clip, f = divmod(g, FRAMES)

        def conv(weights, stack, per_frame):
            depth = per_frame * min(f + 1, 3)
            start = (FRAMES - 1 - f) * per_frame
            right = stack[clip % 2, start : start + depth, 2 * p * LANES : 2 * (p + 1) * LANES]
            if depth % LANES:
                right = jnp.concatenate([right, jnp.zeros((-depth % LANES, 2 * LANES), stack.dtype)], 0)
            return mm(weights[:, : right.shape[0]], right)

        total[p] = conv(mid_ref, s_high, 3 * ch) + conv(mend_ref, s_mend, 6 * ch) * 2.0**-24

    def settle(g, p):
        clip, f = divmod(g, FRAMES)
        for r in range(2):
            h = 2 * p + r
            cell = total[p, :, r * LANES : (r + 1) * LANES]
            mixed = kept[clip % 2 * FRAMES + f, :, h * LANES : (h + 1) * LANES] + cell[ch : 2 * ch]
            mixed = mixed + pltpu.roll(cell[:ch], 1, 1) + pltpu.roll(cell[2 * ch :], LANES - 1, 1)
            act_high, act_low = halves(active(mixed, cols_ref[2], None))
            for part, act in enumerate((act_high, act_high, act_low)):
                at = (2 * part + r) * ch
                last[at : at + ch, p * LANES : (p + 1) * LANES] = act

    def finish(g):
        latent = mm(head_ref[...], last[...])
        lat_high, lat_low = halves(jnp.where(on_phase, latent, 0.0))
        tokens = lax.dot_general(
            fold_ref[...], jnp.concatenate([lat_high, lat_low], 1), NT, preferred_element_type=F32
        )
        for n in range(wide // 4):
            tokens_ref[g, :, n * LANES : (n + 1) * LANES] = tokens[2 * n : 2 * n + 2]
        pltpu.make_async_copy(tokens_ref.at[g], out_any.at[g], sems.at[g]).start()

    last[6 * ch :, :] = ones
    gather(0)
    enter(0, 0)
    enter(0, 1)
    activate(0, range(6))
    for g in range(frames_all):
        after = g + 1
        more = after < frames_all
        if more and after % FRAMES == 0:
            gather(after // FRAMES)
        if more and after % 2 == 0:
            enter(after, 0)
        convolve(g, 0)
        if more and after % 2 == 0:
            enter(after, 1)
        if more:
            activate(after, range(3))
        if g:
            settle(g - 1, 1)
            finish(g - 1)
        convolve(g, 1)
        if more:
            activate(after, range(3, 6))
        settle(g, 0)
    settle(frames_all - 1, 1)
    finish(frames_all - 1)
    for g in range(frames_all):
        pltpu.make_async_copy(tokens_ref.at[g], out_any.at[g], sems.at[g]).wait()


def body(
    loaded, tile_rows, bucket_ids, in_weight, in_bias, bucket_bias, norm_gain, mid_weight, mid_bias, head_gain,
    head_weight, head_bias,
):
    groups_dp = lax.axis_size("dp")
    groups_seq = lax.axis_size("seq")
    row_len = loaded.shape[2] // 2
    wide = row_len // groups_seq
    clips = bucket_ids.shape[0]
    frames_all = clips * FRAMES
    ch = norm_gain.shape[0]
    devices = groups_dp * groups_seq
    deep, deep_mend = 3 * ch, 6 * ch
    vmem = pl.BlockSpec(memory_space=pltpu.VMEM)
    place = pl.BlockSpec(memory_space=pl.ANY)
    part = pltpu.CompilerParams(vmem_limit_bytes=40 * 1024 * 1024)
    whole = pltpu.CompilerParams(vmem_limit_bytes=60 * 1024 * 1024)

    message = pl.pallas_call(
        functools.partial(send_kernel, groups_dp, groups_seq, row_len),
        out_shape=jax.ShapeDtypeStruct((devices, 4, 3 * LANES), F32),
        in_specs=[place] * 2,
        out_specs=vmem,
        scratch_shapes=[
            pltpu.VMEM((TILES, 1, 2 * row_len), F32),
            pltpu.SMEM((1, TILES), jnp.int32),
            pltpu.SemaphoreType.DMA((2,)),
        ],
        compiler_params=whole,
        name="send_windows",
    )(loaded.transpose(1, 0, 2), tile_rows)
    message, bucket_ids = lax.optimization_barrier((message, bucket_ids))
    arrived = lax.all_to_all(message, ("dp", "seq"), split_axis=0, concat_axis=0, tiled=True)

    fold_rows = -(-(wide // 2) // 16) * 16
    zch = head_bias.shape[0]
    small = (
        bucket_ids, in_bias[None], bucket_bias, norm_gain[None], mid_bias[None], head_gain[None], head_weight,
        head_bias[None],
    )
    held = [pltpu.SMEM(bucket_ids.shape, jnp.int32)] + [pltpu.VMEM(op.shape, F32) for op in small[1:]]
    vectors = pl.pallas_call(
        functools.partial(collect_kernel, clips),
        out_shape=jax.ShapeDtypeStruct((16 + zch, LANES), F32),
        in_specs=[place] * len(small),
        out_specs=vmem,
        scratch_shapes=held + [pltpu.SemaphoreType.DMA((len(small),))],
        compiler_params=whole,
        name="collect_vectors",
    )(*small)
    weights = pl.pallas_call(
        functools.partial(prep_kernel, clips, wide),
        out_shape=(
            jax.ShapeDtypeStruct((2, 3 * ch, 4 * LANES), BF16),
            jax.ShapeDtypeStruct((3 * ch, -(-3 * deep // LANES) * LANES), BF16),
            jax.ShapeDtypeStruct((3 * ch, -(-3 * deep_mend // LANES) * LANES), F8),
            jax.ShapeDtypeStruct((LANES, 6 * ch + 64), BF16),
            jax.ShapeDtypeStruct((3, ch, LANES), F32),
            jax.ShapeDtypeStruct((fold_rows, 4 * LANES), BF16),
        ),
        in_specs=[vmem] * 3,
        out_specs=(vmem,) * 6,
        compiler_params=part,
        name="prepare_weights",
    )(vectors, in_weight.T, mid_weight)
    sides = min(clips, 2)
    return pl.pallas_call(
        functools.partial(main_kernel, clips, groups_dp, row_len),
        out_shape=jax.ShapeDtypeStruct((frames_all, 2, wide * 32), F32),
        in_specs=[vmem] * 7,
        out_specs=place,
        scratch_shapes=[
            pltpu.VMEM((frames_all * 24, 2 * LANES), F32),
            pltpu.VMEM((sides, 2, (FRAMES + 2) * SLOT, LANES), BF16),
            pltpu.VMEM((sides, 2, (FRAMES + 2) * SLOT, LANES), BF16),
            pltpu.VMEM((sides, FRAMES * deep, 4 * LANES), BF16),
            pltpu.VMEM((sides, FRAMES * deep_mend, 4 * LANES), F8),
            pltpu.VMEM((sides * FRAMES, ch, 4 * LANES), F32),
            pltpu.VMEM((2, 3 * ch, 2 * LANES), F32),
            pltpu.VMEM((2, 3 * ch, 2 * LANES), F32),
            pltpu.VMEM((6 * ch + 64, 2 * LANES), BF16),
            pltpu.VMEM((frames_all, 2, wide * 32), F32),
            pltpu.SemaphoreType.DMA((frames_all,)),
        ],
        compiler_params=part,
        name="encode_columns",
    )(arrived, *weights)


def solution(mesh):
    return jax.shard_map(
        body,
        mesh=mesh,
        in_specs=(P("seq", "dp", None), P("seq", "dp")) + (P(),) * 10,
        out_specs=P(None, "dp", "seq"),
        check_vma=False,
    )
```

time: 29.3 us -> 27.1 us (0.925)
  local copies, waits for them, and re-layouts: 7.41 us -> 2.82 us
  waiting for transfers between devices: 0.08 us -> 3.47 us
  Pallas kernels: 14 us -> 13.2 us
    unnamed x20 -> x6, local copies, waits for them, and re-layouts: 7.41 us -> 2.82 us
    all_to_all x1, waiting for transfers between devices: 0.08 us -> 3.47 us  [body(): lax.all_to_all(message, ('dp', 'seq'), split_axis=0, concat_axis=0, tiled...]
    pallas_call x1, Pallas kernels: 10.7 us -> 8.67 us  [body(): pl.pallas_call(functools.partial(main_kernel, clips, groups_dp, row_len),...]
    pallas_call x0 -> x1, Pallas kernels: none -> 1.46 us  [body(): pl.pallas_call(functools.partial(collect_kernel, clips), out_shape=jax.Sh...]
  transfers between devices with their start and end apart: 1 -> 1, of which waited for: 1 -> 1; matrix products, arithmetic and copies ran while one was open for 0% -> 0% of each run, Pallas kernels for 6% -> 11%
where the time goes in v2:
time: 27.1 us; the launch traced here: 26.7 us
  Pallas kernels  13.2 us (49%)
  starting transfers between devices  7.1 us (26%)
  waiting for transfers between devices  3.47 us (13%)
  local copies, waits for them, and re-layouts  2.82 us (10%)
    pallas_call x1, Pallas kernels, body(): pl.pallas_call(functools.partial(main_kernel, clips, groups_dp, row_len),...  8.67 us
    all_to_all x1, starting transfers between devices, body(): lax.all_to_all(message, ('dp', 'seq'), split_axis=0, concat_axis=0, tiled...  7.1 us
    all_to_all x1, waiting for transfers between devices, body(): lax.all_to_all(message, ('dp', 'seq'), split_axis=0, concat_axis=0, tiled...  3.47 us
    unnamed x6, local copies, waits for them, and re-layouts  2.82 us
    pallas_call x1, Pallas kernels, body(): pl.pallas_call(functools.partial(send_kernel, groups_dp, groups_seq, row_...  1.6 us
    pallas_call x1, Pallas kernels, body(): pl.pallas_call(functools.partial(prep_kernel, clips, wide), out_shape=(ja...  1.52 us
    pallas_call x1, Pallas kernels, body(): pl.pallas_call(functools.partial(collect_kernel, clips), out_shape=jax.Sh...  1.46 us
  transfers between devices with their start and end apart: 1, of which 1 were waited for; matrix products, arithmetic and copies ran while one was open for 0% of the time, Pallas kernels for 11%

profile of v2, /device:TPU:1, one launch (start us, length us, event | category | flops | bytes accessed | tf_op | source)
XLA Modules:
  0.0 26.7 jit_solution(5917222476301701724)
XLA Ops:
  0.0 1.6 %send_windows.1 = f32[32,4,384]{2,1,0:T(4,128)} custom-call(f32[6,1,1664]{2,1,0:T(1,128)} %bitcast.8, s32[1,6]{1,0:T(1,128)} %tiles_any.1), custom_call_target="tpu_custom_call" | custom-call | tf_op jit(solution)/shard_map/send_windows/pallas_call | solution.py:354
  1.6 7.1 %all-to-all-start = ((f32[32,4,384]{2,1,0:T(4,128)}), f32[32,4,384]{2,1,0:T(4,128)S(1)}, u32[]{:S(2)}, u32[]{:S(2)}) async-start(f32[32,4,384]{2,1,0:T(4,128)} %send_windows.1), calls=%async_computation | async-start | bytes 393216 | tf_op jit(solution)/shard_map/all_to_all | solution.py:368
  8.7 1.5 %collect_vectors.1.vectors_ref = f32[32,128]{1,0:T(8,128)} custom-call(s32[2]{0:T(128)} %refs_0_, f32[1,96]{1,0:T(1,128)} %bitcast.9, f32[4,96]{1,0:T(4,128)} %refs_2_.1, f32[1,96]{1,0:T(1,128)} %bitcast.10, f32[1,96]{1,0:T(1,128)} %bitcast.11, f32[1,96]{1,0:T(1,128)} %bitcast.12, f32[16,96]{1,0:T(8,128)} %refs_6_.1, f32[1,16]{1,0:T(1,128)} %bitcast.13), custom_call_target="tpu_custom_call" | custom-call | tf_op jit(solution)/shard_map/collect_vectors/pallas_call | solution.py:377
  10.2 0.0 copy-start
  10.2 1.3 %copy-done = f32[27,96,96]{2,1,0:T(8,128)S(1)} copy-done((f32[27,96,96]{2,1,0:T(8,128)S(1)}, f32[27,96,96]{2,1,0:T(8,128)}, u32[]{:S(2)}) %copy-start) | copy-done | bytes 995352
  11.5 0.0 copy-start.1
  11.5 0.7 %copy-done.1 = f32[32,128]{1,0:T(8,128)S(1)} copy-done((f32[32,128]{1,0:T(8,128)S(1)}, f32[32,128]{1,0:T(8,128)}, u32[]{:S(2)}) %copy-start.1) | copy-done | bytes 16408
  12.2 0.0 copy-start.2
  12.2 0.8 %copy-done.2 = f32[96,81]{0,1:T(8,128)S(1)} copy-done((f32[96,81]{0,1:T(8,128)S(1)}, f32[96,81]{0,1:T(8,128)}, u32[]{:S(2)}) %copy-start.2) | copy-done | bytes 31128
  13.0 1.5 %prepare_weights.1 = (bf16[2,288,512]{2,1,0:T(8,128)(2,1)S(1)}, bf16[288,896]{1,0:T(8,128)(2,1)S(1)}, f8e4m3fn[288,1792]{1,0:T(32,128)(4,1)S(1)}, bf16[128,640]{...) custom-call(f32[32,128]{1,0:T(8,128)S(1)} %copy-done.1, f32[81,96]{1,0:T(8,128)S(1)} %bitcast.7, ...), custom_call_target="tpu_custom_call" | custom-call | tf_op jit(solution)/shard_map/prepare_weights/pallas_call | solution.py:386
  14.5 3.5 %all-to-all-done.recv_ref = f32[32,4,384]{2,1,0:T(4,128)S(1)} async-done(((f32[32,4,384]{2,1,0:T(4,128)}), f32[32,4,384]{2,1,0:T(4,128)S(1)}, u32[]{:S(2)}, u32[]{:S(2)}) %all-to-all-start) | async-done | bytes 196640 | tf_op jit(solution)/shard_map/all_to_all | solution.py:368
  18.0 8.7 %encode_columns.1 = f32[8,2,3328]{2,1,0:T(2,128)} custom-call(f32[32,4,384]{2,1,0:T(4,128)S(1)} %all-to-all-done.recv_ref, bf16[2,288,512]{2,1,0:T(8,128)(2,1)S(1)} %get-tuple-element.15.entry_ref, bf16[288,896]{1,0:T(8,128)(2,1)S(1)} %get-tuple-element.16.mid_ref, f8e4m3fn[288,1792]{1,0:T(32,128)(4,1)S(1)} %get-tuple-element.17.mend_ref, ...), custom_call_target="tpu_custom_call" | custom-call | tf_op jit(solution)/shard_map/encode_columns/pallas_call | solution.py:402
Async XLA Ops:
  1.6 16.4 %all-to-all-start = ((f32[32,4,384]{2,1,0:T(4,128)}), f32[32,4,384]{2,1,0:T(4,128)S(1)}, u32[]{:S(2)}, u32[]{:S(2)}) async-start(f32[32,4,384]{2,1,0:T(4,128)} %send_windows.1), calls=%async_computation | async-start | bytes 393216 | tf_op jit(solution)/shard_map/all_to_all | solution.py:368
  10.2 1.3 %copy-start = (f32[27,96,96]{2,1,0:T(8,128)S(1)}, f32[27,96,96]{2,1,0:T(8,128)}, u32[]{:S(2)}) copy-start(f32[27,96,96]{2,1,0:T(8,128)} %mid_weight_ref.1) | copy-start | bytes 2985988
  11.5 0.7 %copy-start.1 = (f32[32,128]{1,0:T(8,128)S(1)}, f32[32,128]{1,0:T(8,128)}, u32[]{:S(2)}) copy-start(f32[32,128]{1,0:T(8,128)} %collect_vectors.1.vectors_ref) | copy-start | bytes 49156
  12.2 0.8 %copy-start.2 = (f32[96,81]{0,1:T(8,128)S(1)}, f32[96,81]{0,1:T(8,128)}, u32[]{:S(2)}) copy-start(f32[96,81]{0,1:T(8,128)} %param.15) | copy-start | bytes 93316
